TPU v7x, 32 devices: a whole 2x2x4 slice. The times are simulated.
32 devices in a mesh: attn: 2 (over z_hi), expert: 4 (over y, core), hidden: 2 (over x), pair: 2 (over z_lo).
Axes of the slice: x: 2, y: 2, z: 4 (z_hi: 2, z_lo: 2; z = z_hi * 2 + z_lo), core: 2. Of those that a mesh axis runs over, the one named last changes fastest.
Arguments:
- queries: bfloat16 [8, 128, 512], P(('expert', 'pair'), None, ('attn', 'hidden')), may hold values from -5 to 5
- keys: bfloat16 [8, 128, 256], P(('expert', 'pair'), None, 'attn'), may hold values from -5 to 5
- values: bfloat16 [8, 128, 256], P(('expert', 'pair'), None, 'attn'), may hold values from -6 to 6
- out_weight: bfloat16 [512, 4096], P(('attn', 'hidden')), may hold values from -0.25 to 0.25
- residual: bfloat16 [8, 128, 4096], P(('expert', 'pair'), ('attn', 'hidden')), may hold values from -4 to 4
- norm_gain: float32 [4096], replicated, may hold values from 0.1 to 1.9
- route_logits: float32 [8, 128, 2], P(('expert', 'pair'), ('attn', 'hidden')), may hold values from -6 to 6
- expert_ids: int32 [8, 128, 2], P(('expert', 'pair'), ('attn', 'hidden')), may hold values from 0 to 3, all different within a row; in each aligned block of 32 rows (0 to 31, 32 to 63, ..., all dimensions but the last counted through in order) at most 16 rows name the same one
- doc_lengths: int32 [8, 2], P(('expert', 'pair')), may hold values from 32 to 96, as said below
- gate_up_weight: bfloat16 [4, 2, 4096, 8192], P('expert', None, None, ('attn', 'hidden', 'pair')), may hold values from -0.09375 to 0.09375
- down_weight: bfloat16 [4, 8192, 4096], P('expert', 'attn', ('hidden', 'pair')), may hold values from -0.0625 to 0.0625
Outputs:
- layer_out: bfloat16 [8, 128, 4096], P(('expert', 'pair'), ('attn', 'hidden'))
Inputs may be any that keep to these rules, and one draw needn't show every extreme that they name: `expert_ids`: A token names two different experts; in every aligned block of 32 tokens (all leading dimensions taken together, in order) no expert is named by more than 16 tokens, and in some block one expert is named by exactly 16 tokens. `doc_lengths`: each group has one document of 96 tokens and one of 32 tokens, in either order.
All inputs are finite; a program needn't handle non-finite values.
Results may differ from a plain program's by a relative error of at most 0.022.
Values may be sent and summed in bfloat16 or wider, within the bound.
A program may use at most 64 MiB of HBM per device.

v0:
```python
import jax
import jax.numpy as jnp
from jax import lax
from jax.sharding import PartitionSpec as P

D = 4096
HD = 128


epsilon = 1e-05


def rank_rows(chosen):
    row_total = chosen.shape[-1]
    row_ids = jnp.arange(row_total, dtype=jnp.int32)
    earlier = row_ids[None, :] < row_ids[:, None]
    same_expert = chosen[..., :, None] == chosen[..., None, :]
    return jnp.sum((same_expert & earlier).astype(jnp.int32), axis=-1)


def body(
    queries,
    keys,
    values,
    out_weight,
    residual,
    norm_gain,
    route_logits,
    expert_ids,
    doc_lengths,
    gate_up_weight,
    down_weight,
):
    tok_group = queries.shape[1]
    doc_ends = jnp.cumsum(doc_lengths[0])
    positions = jnp.arange(tok_group, dtype=jnp.int32)
    document = jnp.sum((positions[:, None] >= doc_ends[None, :]).astype(jnp.int32), axis=1)
    allowed = (document[:, None] == document[None, :]) & (positions[None, :] <= positions[:, None])
    scores = jnp.dot(queries[0], keys[0].T, preferred_element_type=jnp.float32) * HD ** (-0.5)
    scores = jnp.where(allowed, scores, -1e30)
    row_top = jnp.max(scores, axis=1, keepdims=True)
    weights = jnp.exp(scores - row_top)
    probabilities = (weights / jnp.sum(weights, axis=1, keepdims=True)).astype(jnp.bfloat16)
    heads_out = jnp.dot(probabilities, values[0], preferred_element_type=jnp.float32).astype(
        jnp.bfloat16
    )
    owned_rows = tok_group // lax.axis_size(("attn", "hidden"))
    subset = heads_out
    owned = lax.psum_scatter(
        jnp.dot(subset, out_weight, preferred_element_type=jnp.float32).astype(jnp.bfloat16),
        ("attn", "hidden"),
        scatter_dimension=0,
        tiled=True,
    ).astype(jnp.float32)
    attended = residual[0].astype(jnp.float32) + owned
    scale = lax.rsqrt(jnp.mean(attended * attended, axis=1, keepdims=True) + epsilon)
    normed = (attended * scale * norm_gain).astype(jnp.bfloat16)
    expert_count = lax.axis_size("expert")
    row_total = 2 * owned_rows
    capacity = max(2, (row_total + expert_count - 1) // expert_count)
    chosen = expert_ids[0].reshape(row_total)
    ranking = rank_rows(chosen)
    targets = jnp.arange(expert_count * capacity, dtype=jnp.int32)
    expert_of_slot = targets // capacity
    rank_of_slot = targets % capacity
    selector = (
        (chosen[None, :] == expert_of_slot[:, None]) & (ranking[None, :] == rank_of_slot[:, None])
    ).astype(jnp.bfloat16)
    repeated = jnp.repeat(normed, 2, axis=0)
    outgoing = jnp.dot(selector, repeated, preferred_element_type=jnp.float32).astype(jnp.bfloat16)
    outgoing = outgoing.reshape(expert_count, capacity, D)
    arrived = lax.all_to_all(outgoing, "expert", split_axis=0, concat_axis=0, tiled=True).reshape(
        expert_count * capacity, D
    )
    gate_up = jnp.einsum(
        "rd,gdf->rgf",
        lax.all_gather(arrived, ("attn", "hidden", "pair"), axis=0, tiled=True),
        gate_up_weight[0],
        preferred_element_type=jnp.float32,
    )
    activated = (jax.nn.silu(gate_up[:, 0]) * gate_up[:, 1]).astype(jnp.bfloat16)
    block_units = lax.all_gather(activated, ("hidden", "pair"), axis=1, tiled=True)
    down_local = down_weight[0]
    subset = block_units
    expert_out = lax.psum_scatter(
        jnp.dot(subset, down_local, preferred_element_type=jnp.float32).astype(jnp.bfloat16),
        "attn",
        scatter_dimension=0,
        tiled=True,
    )
    column_width = expert_out.shape[1]
    pair_count = lax.axis_size(("hidden", "pair"))
    tile_grid = expert_out.reshape(pair_count, expert_count, capacity, column_width)
    outgoing_wide = tile_grid.transpose(1, 0, 2, 3).reshape(
        expert_count * pair_count, 1, capacity, column_width
    )
    returned = lax.all_to_all(
        outgoing_wide, ("expert", "hidden", "pair"), split_axis=0, concat_axis=1, tiled=True
    )
    returned = returned.reshape(expert_count, pair_count, capacity, column_width).transpose(
        0, 2, 1, 3
    )
    returned = returned.reshape(expert_count * capacity, D)
    per_row = jnp.einsum(
        "sr,sd->rd", selector, returned, preferred_element_type=jnp.float32
    ).reshape(owned_rows, 2, D)
    logits = route_logits[0]
    first_share = jax.nn.sigmoid(logits[:, 0] - logits[:, 1])
    layer_out = (
        attended
        + first_share[:, None] * per_row[:, 0]
        + (1.0 - first_share)[:, None] * per_row[:, 1]
    )
    return layer_out.astype(jnp.bfloat16)[None]


def solution(mesh):
    in_specs = (
        P(("expert", "pair"), None, ("attn", "hidden")),
        P(("expert", "pair"), None, "attn"),
        P(("expert", "pair"), None, "attn"),
        P(("attn", "hidden"), None),
        P(("expert", "pair"), ("attn", "hidden"), None),
        P(),
        P(("expert", "pair"), ("attn", "hidden"), None),
        P(("expert", "pair"), ("attn", "hidden"), None),
        P(("expert", "pair"), None),
        P("expert", None, None, ("attn", "hidden", "pair")),
        P("expert", "attn", ("hidden", "pair")),
    )
    out_specs = P(("expert", "pair"), ("attn", "hidden"), None)
    return jax.shard_map(body, mesh=mesh, in_specs=in_specs, out_specs=out_specs, check_vma=False)
```

profile of v0, /device:TPU:9, one launch (start us, length us, event | category | flops | bytes accessed | tf_op | source)
XLA Modules:
  0.0 307.3 jit_solution(8228485448514632945)
XLA Ops:
  6.5 0.0 copy-start
  6.5 0.0 copy-start.1
  6.5 0.0 reduce-scatter.3.cloned.1.call-start
  6.5 0.9 reduce-window.8
  7.5 0.1 fusion.43
  7.6 1.0 fusion.44
  8.6 0.0 copy-done
  8.6 2.3 convolution_convert_fusion
  10.9 0.0 reduce-scatter.3.cloned.1.call-update
  10.9 0.0 all-gather.3.cloned.1.call-start
  11.0 0.8 copy.23
  11.7 0.1 eq.89
  11.9 0.2 convert_reduce_fusion
  12.0 33.1 %reduce-scatter.3.cloned.1.call-done = bf16[32,4096]{1,0:T(8,128)(2,1)} async-done(((bf16[128,4096]{1,0:T(8,128)(2,1)}), bf16[32,4096]{1,0:T(8,128)(2,1)}) %reduce-scatter.3.cloned.1.call-update) | async-done | bytes 262160 | tf_op jit(solution)/shard_map/reduce_scatter | solution.py:49
  45.2 1.2 multiply_reduce_fusion
  46.4 0.0 copy-done.1
  46.4 1.1 multiply_convert_fusion
  47.5 0.5 broadcast_in_dim.9
  48.0 0.2 reshape.116
  48.2 0.4 convolution_convert_fusion.1
  48.5 11.6 %all_to_all.14 = bf16[4,16,4096]{2,1,0:T(8,128)(2,1)} all-to-all(bf16[4,16,4096]{2,1,0:T(8,128)(2,1)S(1)} %bitcast.86), channel_id=1, replica_groups=mesh['attn'=2,'expert'=4,'hidden'=2,'pair'=2] {'expert'}, dimensions={0} | all-to-all | bytes 1048576 | tf_op jit(solution)/shard_map/all_to_all | solution.py:72
  60.1 0.0 all-gather.3.cloned.1.call-update
  60.2 0.0 all-gather.5.cloned.1.call-start
  60.2 88.4 %all-gather.3.cloned.1.call-done = bf16[512,4096]{1,0:T(8,128)(2,1)} async-done(((bf16[64,4096]{1,0:T(8,128)(2,1)}), bf16[512,4096]{1,0:T(8,128)(2,1)}) %all-gather.3.cloned.1.call-update) | async-done | bytes 4194320 | tf_op jit(solution)/shard_map/all_gather | solution.py:77
  148.6 13.0 %fusion = f32[512,2,1024]{2,0,1:T(8,128)S(1)} fusion(bf16[1,2,4096,1024]{3,2,1,0:T(8,128)(2,1)} %param.20, bf16[512,4096]{1,0:T(8,128)(2,1)} %all-gather.3.cloned.1.call-done), kind=kOutput, calls=%fused_computation | convolution fusion | flops 8589934592 | bytes 25165824 | tf_op jit(solution)/shard_map/rd,gdf->rgf/dot_general | solution.py:75
  161.6 1.6 fusion.6
  163.2 0.0 all-gather.5.cloned.1.call-update
  163.2 0.0 copy-start.4
  163.2 0.0 reduce-scatter.5.cloned.1.call-start
  163.3 78.2 %all-gather.5.cloned.1.call-done = bf16[512,4096]{1,0:T(8,128)(2,1)} async-done(((bf16[512,1024]{1,0:T(8,128)(2,1)}), bf16[512,4096]{1,0:T(8,128)(2,1)}) %all-gather.5.cloned.1.call-update) | async-done | bytes 4194320 | tf_op jit(solution)/shard_map/all_gather | solution.py:82
  241.5 10.1 %fusion.7 = bf16[512,1024]{1,0:T(8,128)(2,1)} fusion(bf16[512,4096]{1,0:T(8,128)(2,1)} %all-gather.5.cloned.1.call-done, bf16[1,4096,1024]{2,1,0:T(8,128)(2,1)} %param.21), kind=kOutput, calls=%fused_computation.11 | convolution fusion | flops 4295491584 | bytes 13631488 | tf_op jit(solution)/shard_map/dot_general | solution.py:86
  251.6 0.0 copy-start.3
  251.6 0.0 copy-start.2
  251.7 0.0 reduce-scatter.5.cloned.1.call-update
  251.7 28.8 %reduce-scatter.5.cloned.1.call-done = bf16[256,1024]{1,0:T(8,128)(2,1)} async-done(((bf16[512,1024]{1,0:T(8,128)(2,1)}), bf16[256,1024]{1,0:T(8,128)(2,1)}) %reduce-scatter.5.cloned.1.call-update) | async-done | bytes 524304 | tf_op jit(solution)/shard_map/reduce_scatter | solution.py:85
  280.5 1.9 copy.25
  282.4 8.4 %all-to-all-start.1 = ((bf16[16,1,16,1024]{3,2,1,0:T(8,128)(2,1)}), bf16[16,1,16,1024]{3,2,1,0:T(8,128)(2,1)S(1)}, u32[]{:S(2)}, u32[]{:S(2)}) async-start(bf16[16,1,16,1024]{3,2,1,0:T(8,128)(2,1)} %bitcast.19), calls=%async_computation.3 | async-start | bytes 1048576 | tf_op jit(solution)/shard_map/all_to_all | solution.py:97
  290.8 0.1 eq.93
  290.9 0.1 copy.24
  291.0 0.0 copy-done.4
  291.0 7.8 %all-to-all-done.1 = bf16[16,1,16,1024]{3,2,1,0:T(8,128)(2,1)S(1)} async-done(((bf16[16,1,16,1024]{3,2,1,0:T(8,128)(2,1)}), bf16[16,1,16,1024]{3,2,1,0:T(8,128)(2,1)S(1)}, u32[]{:S(2)}, u32[]{:S(2)}) %all-to-all-start.1) | async-done | bytes 524320 | tf_op jit(solution)/shard_map/all_to_all | solution.py:97
  298.8 0.4 copy.27
  299.2 0.4 reshape.125
  299.5 0.0 copy-done.3
  299.6 0.4 fusion.31
  299.9 0.0 copy-done.2
  299.9 0.9 fusion.16
  (4 shorter events, 0.1 us)
Async XLA Ops:
  6.5 2.0 copy-start
  6.5 39.9 %copy-start.1 = (bf16[1,32,4096]{2,1,0:T(8,128)(2,1)S(1)}, bf16[1,32,4096]{2,1,0:T(8,128)(2,1)}, u32[]{:S(2)}) copy-start(bf16[1,32,4096]{2,1,0:T(8,128)(2,1)} %param.15) | copy-start | bytes 786436
  6.5 38.6 %reduce-scatter.3.cloned.1.call-start = ((), (), s32[]{:S(2)}) async-start(), calls=%async_computation.4 | async-start | bytes 1310720 | tf_op jit(solution)/shard_map/reduce_scatter | solution.py:49
  10.9 137.7 %all-gather.3.cloned.1.call-start = ((), (), s32[]{:S(2)}) async-start(), calls=%async_computation.5 | async-start | bytes 4718592 | tf_op jit(solution)/shard_map/all_gather | solution.py:77
  60.2 181.4 %all-gather.5.cloned.1.call-start = ((), (), s32[]{:S(2)}) async-start(), calls=%async_computation.6 | async-start | bytes 5242880 | tf_op jit(solution)/shard_map/all_gather | solution.py:82
  163.2 127.8 %copy-start.4 = (f32[1,32,2]{1,2,0:T(2,128)S(1)}, f32[1,32,2]{1,2,0:T(2,128)}, u32[]{:S(2)}) copy-start(f32[1,32,2]{1,2,0:T(2,128)} %param.17) | copy-start | bytes 772
  163.2 117.3 %reduce-scatter.5.cloned.1.call-start = ((), (), s32[]{:S(2)}) async-start(), calls=%async_computation.7 | async-start | bytes 1572864 | tf_op jit(solution)/shard_map/reduce_scatter | solution.py:85
  251.6 47.9 %copy-start.3 = (s32[1,32,2]{1,2,0:T(2,128)S(1)}, s32[1,32,2]{1,2,0:T(2,128)}, u32[]{:S(2)}) copy-start(s32[1,32,2]{1,2,0:T(2,128)} %param.18) | copy-start | bytes 772
  251.6 48.3 %copy-start.2 = (bf16[32,4096]{1,0:T(8,128)(2,1)S(1)}, bf16[32,4096]{1,0:T(8,128)(2,1)}, u32[]{:S(2)}) copy-start(bf16[32,4096]{1,0:T(8,128)(2,1)} %reduce-scatter.3.cloned.1.call-done) | copy-start | bytes 786436
  282.4 16.3 %all-to-all-start.1 = ((bf16[16,1,16,1024]{3,2,1,0:T(8,128)(2,1)}), bf16[16,1,16,1024]{3,2,1,0:T(8,128)(2,1)S(1)}, u32[]{:S(2)}, u32[]{:S(2)}) async-start(bf16[16,1,16,1024]{3,2,1,0:T(8,128)(2,1)} %bitcast.19), calls=%async_computation.3 | async-start | bytes 1048576 | tf_op jit(solution)/shard_map/all_to_all | solution.py:97
Sparse Core Ops, SparseCore 0:
  11.0 34.0 reduce-scatter.2
  60.3 88.3 all-gather.2
  163.3 78.1 all-gather.4
  251.8 28.6 reduce-scatter.4
where the time goes:
time: 310 us; the launch traced here: 307 us
  waiting for transfers between devices  236 us (76%)
  matrix products  27.1 us (9%)
  between operations  13.2 us (4%)
  blocking collectives  11.6 us (4%)
  starting transfers between devices  8.5 us (3%)
  other arithmetic  6.01 us (2%)
  local copies, waits for them, and re-layouts  4.41 us (1%)
    all_gather x1, waiting for transfers between devices, body(): lax.all_gather(arrived, ('attn', 'hidden', 'pair'), axis=0, tiled=True)  88.4 us
    all_gather x1, waiting for transfers between devices, body(): lax.all_gather(activated, ('hidden', 'pair'), axis=1, tiled=True)  78.2 us
    reduce_scatter x1, waiting for transfers between devices, body(): lax.psum_scatter(jnp.dot(subset, out_weight, preferred_element_type=jnp.f...  33.1 us
    reduce_scatter x1, waiting for transfers between devices, body(): lax.psum_scatter(jnp.dot(subset, down_local, preferred_element_type=jnp.f...  28.8 us
    dot_general x1, matrix products, body(): jnp.einsum('rd,gdf->rgf', lax.all_gather(arrived, ('attn', 'hidden', 'pai...  13 us
    all_to_all x1, blocking collectives, body(): lax.all_to_all(outgoing, 'expert', split_axis=0, concat_axis=0, tiled=True)  11.6 us
    dot_general x1, matrix products, body(): jnp.dot(subset, down_local, preferred_element_type=jnp.float32)  10.1 us
    all_to_all x1, starting transfers between devices, body(): lax.all_to_all(outgoing_wide, ('expert', 'hidden', 'pair'), split_axis=0,...  8.37 us
  transfers between devices with their start and end apart: 5, of which 5 were waited for; matrix products, arithmetic and copies ran while one was open for 0% of the time, Pallas kernels for 0%

commit v1 on v0

--- a/solution.py
+++ b/solution.py
@@ -32,7 +32,9 @@
     down_weight,
 ):
     tok_group = queries.shape[1]
-    doc_ends = jnp.cumsum(doc_lengths[0])
+    lengths = doc_lengths[0]
+    order = jnp.arange(lengths.shape[0], dtype=jnp.int32)
+    doc_ends = jnp.sum(jnp.where(order[None, :] <= order[:, None], lengths[None, :], 0), axis=1)
     positions = jnp.arange(tok_group, dtype=jnp.int32)
     document = jnp.sum((positions[:, None] >= doc_ends[None, :]).astype(jnp.int32), axis=1)
     allowed = (document[:, None] == document[None, :]) & (positions[None, :] <= positions[:, None])

time: 310 us -> 310 us (level)
  no operation moved by 1% of the time
where the time goes in v1:
time: 310 us; the launch traced here: 307 us
  waiting for transfers between devices  236 us (76%)
  matrix products  27.1 us (9%)
  between operations  13.2 us (4%)
  blocking collectives  11.6 us (4%)
  starting transfers between devices  8.5 us (3%)
  other arithmetic  5.96 us (2%)
  local copies, waits for them, and re-layouts  4.41 us (1%)
    all_gather x1, waiting for transfers between devices, body(): lax.all_gather(arrived, ('attn', 'hidden', 'pair'), axis=0, tiled=True)  88.4 us
    all_gather x1, waiting for transfers between devices, body(): lax.all_gather(activated, ('hidden', 'pair'), axis=1, tiled=True)  78.2 us
    reduce_scatter x1, waiting for transfers between devices, body(): lax.psum_scatter(jnp.dot(subset, out_weight, preferred_element_type=jnp.f...  33.1 us
    reduce_scatter x1, waiting for transfers between devices, body(): lax.psum_scatter(jnp.dot(subset, down_local, preferred_element_type=jnp.f...  28.8 us
    dot_general x1, matrix products, body(): jnp.einsum('rd,gdf->rgf', lax.all_gather(arrived, ('attn', 'hidden', 'pai...  13 us
    all_to_all x1, blocking collectives, body(): lax.all_to_all(outgoing, 'expert', split_axis=0, concat_axis=0, tiled=True)  11.6 us
    dot_general x1, matrix products, body(): jnp.dot(subset, down_local, preferred_element_type=jnp.float32)  10.1 us
    all_to_all x1, starting transfers between devices, body(): lax.all_to_all(outgoing_wide, ('expert', 'hidden', 'pair'), split_axis=0,...  8.37 us
  transfers between devices with their start and end apart: 5, of which 5 were waited for; matrix products, arithmetic and copies ran while one was open for 0% of the time, Pallas kernels for 0%

profile of v1, /device:TPU:9, one launch (start us, length us, event | category | flops | bytes accessed | tf_op | source)
XLA Modules:
  0.0 307.3 jit_solution(16542750457288445919)
XLA Ops:
  6.5 0.0 copy-start
  6.5 0.0 copy-start.1
  6.5 0.0 reduce-scatter.3.cloned.1.call-start
  6.5 0.9 fusion.43
  7.4 0.1 fusion.44
  7.5 1.0 fusion.45
  8.5 0.0 copy-done
  8.5 2.3 convolution_convert_fusion
  10.9 0.0 reduce-scatter.3.cloned.1.call-update
  10.9 0.0 all-gather.3.cloned.1.call-start
  10.9 0.8 copy.23
  11.7 0.1 eq.89
  11.8 0.2 convert_reduce_fusion
  12.0 33.1 %reduce-scatter.3.cloned.1.call-done = bf16[32,4096]{1,0:T(8,128)(2,1)} async-done(((bf16[128,4096]{1,0:T(8,128)(2,1)}), bf16[32,4096]{1,0:T(8,128)(2,1)}) %reduce-scatter.3.cloned.1.call-update) | async-done | bytes 262160 | tf_op jit(solution)/shard_map/reduce_scatter | solution.py:51
  45.1 1.2 multiply_reduce_fusion
  46.3 0.0 copy-done.1
  46.4 1.1 multiply_convert_fusion
  47.4 0.5 broadcast_in_dim.26
  47.9 0.2 reshape.91
  48.1 0.4 convolution_convert_fusion.1
  48.5 11.6 %all_to_all.14 = bf16[4,16,4096]{2,1,0:T(8,128)(2,1)} all-to-all(bf16[4,16,4096]{2,1,0:T(8,128)(2,1)S(1)} %bitcast.85), channel_id=1, replica_groups=mesh['attn'=2,'expert'=4,'hidden'=2,'pair'=2] {'expert'}, dimensions={0} | all-to-all | bytes 1048576 | tf_op jit(solution)/shard_map/all_to_all | solution.py:74
  60.1 0.0 all-gather.3.cloned.1.call-update
  60.1 0.0 all-gather.5.cloned.1.call-start
  60.2 88.4 %all-gather.3.cloned.1.call-done = bf16[512,4096]{1,0:T(8,128)(2,1)} async-done(((bf16[64,4096]{1,0:T(8,128)(2,1)}), bf16[512,4096]{1,0:T(8,128)(2,1)}) %all-gather.3.cloned.1.call-update) | async-done | bytes 4194320 | tf_op jit(solution)/shard_map/all_gather | solution.py:79
  148.6 13.0 %fusion = f32[512,2,1024]{2,0,1:T(8,128)S(1)} fusion(bf16[1,2,4096,1024]{3,2,1,0:T(8,128)(2,1)} %param.20, bf16[512,4096]{1,0:T(8,128)(2,1)} %all-gather.3.cloned.1.call-done), kind=kOutput, calls=%fused_computation | convolution fusion | flops 8589934592 | bytes 25165824 | tf_op jit(solution)/shard_map/rd,gdf->rgf/dot_general | solution.py:77
  161.6 1.6 fusion.6
  163.1 0.0 all-gather.5.cloned.1.call-update
  163.2 0.0 copy-start.4
  163.2 0.0 reduce-scatter.5.cloned.1.call-start
  163.2 78.2 %all-gather.5.cloned.1.call-done = bf16[512,4096]{1,0:T(8,128)(2,1)} async-done(((bf16[512,1024]{1,0:T(8,128)(2,1)}), bf16[512,4096]{1,0:T(8,128)(2,1)}) %all-gather.5.cloned.1.call-update) | async-done | bytes 4194320 | tf_op jit(solution)/shard_map/all_gather | solution.py:84
  241.5 10.1 %fusion.7 = bf16[512,1024]{1,0:T(8,128)(2,1)} fusion(bf16[512,4096]{1,0:T(8,128)(2,1)} %all-gather.5.cloned.1.call-done, bf16[1,4096,1024]{2,1,0:T(8,128)(2,1)} %param.21), kind=kOutput, calls=%fused_computation.11 | convolution fusion | flops 4295491584 | bytes 13631488 | tf_op jit(solution)/shard_map/dot_general | solution.py:88
  251.6 0.0 copy-start.3
  251.6 0.0 copy-start.2
  251.6 0.0 reduce-scatter.5.cloned.1.call-update
  251.6 28.8 %reduce-scatter.5.cloned.1.call-done = bf16[256,1024]{1,0:T(8,128)(2,1)} async-done(((bf16[512,1024]{1,0:T(8,128)(2,1)}), bf16[256,1024]{1,0:T(8,128)(2,1)}) %reduce-scatter.5.cloned.1.call-update) | async-done | bytes 524304 | tf_op jit(solution)/shard_map/reduce_scatter | solution.py:87
  280.5 1.9 copy.25
  282.4 8.4 %all-to-all-start.1 = ((bf16[16,1,16,1024]{3,2,1,0:T(8,128)(2,1)}), bf16[16,1,16,1024]{3,2,1,0:T(8,128)(2,1)S(1)}, u32[]{:S(2)}, u32[]{:S(2)}) async-start(bf16[16,1,16,1024]{3,2,1,0:T(8,128)(2,1)} %bitcast.18), calls=%async_computation.3 | async-start | bytes 1048576 | tf_op jit(solution)/shard_map/all_to_all | solution.py:99
  290.7 0.1 eq.93
  290.8 0.1 copy.24
  290.9 0.0 copy-done.4
  290.9 7.8 %all-to-all-done.1 = bf16[16,1,16,1024]{3,2,1,0:T(8,128)(2,1)S(1)} async-done(((bf16[16,1,16,1024]{3,2,1,0:T(8,128)(2,1)}), bf16[16,1,16,1024]{3,2,1,0:T(8,128)(2,1)S(1)}, u32[]{:S(2)}, u32[]{:S(2)}) %all-to-all-start.1) | async-done | bytes 524320 | tf_op jit(solution)/shard_map/all_to_all | solution.py:99
  298.7 0.4 copy.27
  299.1 0.4 reshape.100
  299.5 0.0 copy-done.3
  299.5 0.4 fusion.31
  299.9 0.0 copy-done.2
  299.9 0.9 fusion.16
  (4 shorter events, 0.1 us)
Async XLA Ops:
  6.5 2.0 copy-start
  6.5 39.8 %copy-start.1 = (bf16[1,32,4096]{2,1,0:T(8,128)(2,1)S(1)}, bf16[1,32,4096]{2,1,0:T(8,128)(2,1)}, u32[]{:S(2)}) copy-start(bf16[1,32,4096]{2,1,0:T(8,128)(2,1)} %param.15) | copy-start | bytes 786436
  6.5 38.6 %reduce-scatter.3.cloned.1.call-start = ((), (), s32[]{:S(2)}) async-start(), calls=%async_computation.4 | async-start | bytes 1310720 | tf_op jit(solution)/shard_map/reduce_scatter | solution.py:51
  10.9 137.7 %all-gather.3.cloned.1.call-start = ((), (), s32[]{:S(2)}) async-start(), calls=%async_computation.5 | async-start | bytes 4718592 | tf_op jit(solution)/shard_map/all_gather | solution.py:79
  60.1 181.4 %all-gather.5.cloned.1.call-start = ((), (), s32[]{:S(2)}) async-start(), calls=%async_computation.6 | async-start | bytes 5242880 | tf_op jit(solution)/shard_map/all_gather | solution.py:84
  163.2 127.8 %copy-start.4 = (f32[1,32,2]{1,2,0:T(2,128)S(1)}, f32[1,32,2]{1,2,0:T(2,128)}, u32[]{:S(2)}) copy-start(f32[1,32,2]{1,2,0:T(2,128)} %param.17) | copy-start | bytes 772
  163.2 117.3 %reduce-scatter.5.cloned.1.call-start = ((), (), s32[]{:S(2)}) async-start(), calls=%async_computation.7 | async-start | bytes 1572864 | tf_op jit(solution)/shard_map/reduce_scatter | solution.py:87
  251.6 47.9 %copy-start.3 = (s32[1,32,2]{1,2,0:T(2,128)S(1)}, s32[1,32,2]{1,2,0:T(2,128)}, u32[]{:S(2)}) copy-start(s32[1,32,2]{1,2,0:T(2,128)} %param.18) | copy-start | bytes 772
  251.6 48.3 %copy-start.2 = (bf16[32,4096]{1,0:T(8,128)(2,1)S(1)}, bf16[32,4096]{1,0:T(8,128)(2,1)}, u32[]{:S(2)}) copy-start(bf16[32,4096]{1,0:T(8,128)(2,1)} %reduce-scatter.3.cloned.1.call-done) | copy-start | bytes 786436
  282.4 16.3 %all-to-all-start.1 = ((bf16[16,1,16,1024]{3,2,1,0:T(8,128)(2,1)}), bf16[16,1,16,1024]{3,2,1,0:T(8,128)(2,1)S(1)}, u32[]{:S(2)}, u32[]{:S(2)}) async-start(bf16[16,1,16,1024]{3,2,1,0:T(8,128)(2,1)} %bitcast.18), calls=%async_computation.3 | async-start | bytes 1048576 | tf_op jit(solution)/shard_map/all_to_all | solution.py:99
Sparse Core Ops, SparseCore 0:
  11.0 34.0 reduce-scatter.2
  60.2 88.3 all-gather.2
  163.3 78.1 all-gather.4
  251.7 28.6 reduce-scatter.4

commit v2 on v1

--- a/solution.py
+++ b/solution.py
@@ -1,6 +1,10 @@
+import functools
+
 import jax
 import jax.numpy as jnp
 from jax import lax
+from jax.experimental import pallas as pl
+from jax.experimental.pallas import tpu as pltpu
 from jax.sharding import PartitionSpec as P
 
 D = 4096
@@ -18,19 +22,7 @@
     return jnp.sum((same_expert & earlier).astype(jnp.int32), axis=-1)
 
 
-def body(
-    queries,
-    keys,
-    values,
-    out_weight,
-    residual,
-    norm_gain,
-    route_logits,
-    expert_ids,
-    doc_lengths,
-    gate_up_weight,
-    down_weight,
-):
+def attention(queries, keys, values, doc_lengths):
     tok_group = queries.shape[1]
     lengths = doc_lengths[0]
     order = jnp.arange(lengths.shape[0], dtype=jnp.int32)
@@ -46,6 +38,24 @@
     heads_out = jnp.dot(probabilities, values[0], preferred_element_type=jnp.float32).astype(
         jnp.bfloat16
     )
+    return heads_out
+
+
+def plain_body(
+    queries,
+    keys,
+    values,
+    out_weight,
+    residual,
+    norm_gain,
+    route_logits,
+    expert_ids,
+    doc_lengths,
+    gate_up_weight,
+    down_weight,
+):
+    tok_group = queries.shape[1]
+    heads_out = attention(queries, keys, values, doc_lengths)
     owned_rows = tok_group // lax.axis_size(("attn", "hidden"))
     subset = heads_out
     owned = lax.psum_scatter(
@@ -116,6 +126,425 @@
     return layer_out.astype(jnp.bfloat16)[None]
 
 
+def layer_kernel(
+    sizes,
+    heads_ref,
+    out_weight_ref,
+    residual_ref,
+    gain_ref,
+    pick_ref,
+    back_ref,
+    share_ref,
+    gate_up_hbm,
+    down_hbm,
+    out_ref,
+    gate_up_ref,
+    down_ref,
+    part_ref,
+    sums_ref,
+    attended_ref,
+    outgoing_ref,
+    rows_ref,
+    acts_ref,
+    stage_ref,
+    returned_ref,
+    weight_sem,
+    send_sem,
+    recv_sem,
+):
+    n_attn, n_expert, n_hidden, n_pair, own, cap = sizes
+    names = ("attn", "expert", "hidden", "pair")
+    counts = (n_attn, n_expert, n_hidden, n_pair)
+    me = tuple(lax.axis_index(name) for name in names)
+    a, e, h, p = me
+    width = rows_ref.shape[1]
+    units = acts_ref.shape[2]
+    columns = down_ref.shape[1]
+    block = n_expert * cap
+    chunk = n_hidden * block
+    chunks = n_attn * n_pair
+    half = chunk // 2
+    pending = []
+
+    def shifted(offset, sign=1):
+        return tuple(
+            lax.rem(x + (sign * d) % n, n) if d else x for x, d, n in zip(me, offset, counts)
+        )
+
+    def copy(src, dst, sem, target):
+        return pltpu.make_async_remote_copy(
+            src_ref=src,
+            dst_ref=dst,
+            send_sem=send_sem.at[sem],
+            recv_sem=recv_sem.at[sem],
+            device_id=dict(zip(names, target)),
+            device_id_type=pl.DeviceIdType.MESH,
+        )
+
+    def send(src, dst, sem, target):
+        started = copy(src, dst, sem, target)
+        started.start()
+        pending.append(started)
+
+    def arrive(ref, sem):
+        copy(ref, ref, sem, shifted((0, 1, 0, 0))).wait_recv()
+
+    def at(start, size, align=16):
+        return pl.ds(pl.multiple_of(start, align), size)
+
+    weights = [
+        pltpu.make_async_copy(gate_up_hbm.at[0], gate_up_ref, weight_sem.at[0]),
+        pltpu.make_async_copy(down_hbm.at[0], down_ref, weight_sem.at[1]),
+    ]
+    for load in weights:
+        load.start()
+
+    barrier = pltpu.get_barrier_semaphore()
+    others = [
+        (da, de, dh, dp)
+        for da in range(n_attn)
+        for de in range(n_expert)
+        for dh in range(n_hidden)
+        for dp in range(n_pair)
+        if (da, de, dh, dp) != (0, 0, 0, 0)
+    ]
+    for offset in others:
+        pl.semaphore_signal(
+            barrier,
+            inc=1,
+            device_id=dict(zip(names, shifted(offset))),
+            device_id_type=pl.DeviceIdType.MESH,
+        )
+    pl.semaphore_wait(barrier, len(others))
+
+    used = 0
+
+    def numbers(count):
+        nonlocal used
+        used += count
+        return used - count
+
+    first = numbers(n_attn * n_hidden)
+    mine = a * n_hidden + h
+    for da in reversed(range(n_attn)):
+        for dh in reversed(range(n_hidden)):
+            target = shifted((da, 0, dh, 0))
+            owner = target[0] * n_hidden + target[2]
+            partial = jnp.dot(
+                heads_ref[at(owner * own, own), :],
+                out_weight_ref[...],
+                preferred_element_type=jnp.float32,
+            )
+            if da or dh:
+                slot = da * n_hidden + dh
+                part_ref[slot] = partial.astype(jnp.bfloat16)
+                send(part_ref.at[slot], sums_ref.at[mine], first + slot, target)
+            else:
+                attended_ref[...] = partial + residual_ref[0].astype(jnp.float32)
+    for da in range(n_attn):
+        for dh in range(n_hidden):
+            if da or dh:
+                source = shifted((da, 0, dh, 0), -1)
+                slot = source[0] * n_hidden + source[2]
+                arrive(sums_ref.at[slot], first + da * n_hidden + dh)
+                attended_ref[...] += sums_ref[slot].astype(jnp.float32)
+    attended = attended_ref[...]
+    scale = lax.rsqrt(jnp.mean(attended * attended, axis=1, keepdims=True) + epsilon)
+    normed = (attended * scale * gain_ref[...]).astype(jnp.bfloat16)
+    outgoing_ref[...] = jnp.dot(
+        pick_ref[...], normed, preferred_element_type=jnp.float32
+    ).astype(jnp.bfloat16)
+
+    base = ((a * n_pair + p) * n_hidden + h) * block
+    first = numbers(n_expert)
+    for de in reversed(range(1, n_expert)):
+        target = shifted((0, de, 0, 0))
+        send(
+            outgoing_ref.at[at(target[1] * cap, cap)],
+            rows_ref.at[at(base + e * cap, cap)],
+            first + de,
+            target,
+        )
+    rows_ref[at(base + e * cap, cap), :] = outgoing_ref[at(e * cap, cap), :]
+    for de in range(1, n_expert):
+        source = shifted((0, de, 0, 0), -1)
+        arrive(rows_ref.at[at(base + source[1] * cap, cap)], first + de)
+
+    steps = [(da, dp) for da in range(n_attn) for dp in range(n_pair)]
+    along = numbers(chunks)
+    across = numbers(chunks * n_hidden)
+
+    def spread(step, start):
+        for dh in range(1, n_hidden):
+            block_ref = rows_ref.at[at(start, block)]
+            send(block_ref, block_ref, across + step * n_hidden + dh, shifted((0, 0, dh, 0)))
+
+    own_rows = rows_ref.at[at(base, block)]
+    spread(0, base)
+    for step, (da, dp) in enumerate(steps):
+        if step:
+            send(own_rows, own_rows, along + step, shifted((da, 0, 0, dp)))
+
+    def chunk_of(step):
+        da, dp = steps[step]
+        source = shifted((da, 0, 0, dp), -1)
+        return source[0] * n_pair + source[3]
+
+    def forward(step):
+        start = (chunk_of(step) * n_hidden + h) * block
+        arrive(rows_ref.at[at(start, block)], along + step)
+        spread(step, start)
+
+    near = numbers(chunks * n_hidden * 2)
+    side = numbers(chunks * n_pair * 2)
+    turn_side = numbers(chunks * n_hidden * n_pair)
+    turn_near = numbers(chunks * n_hidden * n_pair)
+    group = h * n_pair + p
+
+    def piece(owner, c, part):
+        return acts_ref.at[owner, at(c * chunk + part * half, half)]
+
+    def up(step):
+        c = chunk_of(step)
+        for dh in range(1, n_hidden):
+            source = shifted((0, 0, dh, 0), -1)
+            start = (c * n_hidden + source[2]) * block
+            arrive(rows_ref.at[at(start, block)], across + step * n_hidden + dh)
+        tile = min(256, units)
+
+        @pl.loop(0, units // tile)
+        def _(t):
+            where = at(t * tile, tile, 128)
+            rows = rows_ref[at(c * chunk, chunk), :]
+            gate = jnp.dot(rows, gate_up_ref[0, :, where], preferred_element_type=jnp.float32)
+            upward = jnp.dot(rows, gate_up_ref[1, :, where], preferred_element_type=jnp.float32)
+            acts_ref[group, at(c * chunk, chunk), where] = (
+                gate / (1.0 + jnp.exp(-gate)) * upward
+            ).astype(jnp.bfloat16)
+
+        for part in range(2):
+            mine_ref = piece(group, c, part)
+            for dh in range(1, n_hidden):
+                sem = near + (c * n_hidden + dh) * 2 + part
+                send(mine_ref, mine_ref, sem, shifted((0, 0, dh, 0)))
+            for dp in range(1, n_pair):
+                sem = side + (c * n_pair + dp) * 2 + part
+                send(mine_ref, mine_ref, sem, shifted((0, 0, 0, dp)))
+
+    def turn(step):
+        c = chunk_of(step)
+        for dh in range(1, n_hidden):
+            owner = shifted((0, 0, dh, 0), -1)[2] * n_pair + p
+            landed = piece(owner, c, 0)
+            arrive(landed, near + (c * n_hidden + dh) * 2)
+            for dp in range(1, n_pair):
+                sem = turn_side + (c * n_hidden + dh) * n_pair + dp
+                send(landed, landed, sem, shifted((0, 0, 0, dp)))
+        for dp in range(1, n_pair):
+            owner = h * n_pair + shifted((0, 0, 0, dp), -1)[3]
+            landed = piece(owner, c, 1)
+            arrive(landed, side + (c * n_pair + dp) * 2 + 1)
+            for dh in range(1, n_hidden):
+                sem = turn_near + (c * n_hidden + dh) * n_pair + dp
+                send(landed, landed, sem, shifted((0, 0, dh, 0)))
+
+    last = numbers(n_attn * n_expert * n_hidden * n_pair)
+
+    def number(da, de, dh, dp):
+        return last + ((da * n_expert + de) * n_hidden + dh) * n_pair + dp
+
+    def down(step):
+        c = chunk_of(step)
+        for dh in range(1, n_hidden):
+            owner = shifted((0, 0, dh, 0), -1)[2] * n_pair + p
+            arrive(piece(owner, c, 1), near + (c * n_hidden + dh) * 2 + 1)
+        for dp in range(1, n_pair):
+            owner = h * n_pair + shifted((0, 0, 0, dp), -1)[3]
+            arrive(piece(owner, c, 0), side + (c * n_pair + dp) * 2)
+        for dh in range(1, n_hidden):
+            for dp in range(1, n_pair):
+                source = shifted((0, 0, dh, dp), -1)
+                owner = source[2] * n_pair + source[3]
+                sem = (c * n_hidden + dh) * n_pair + dp
+                arrive(piece(owner, c, 0), turn_side + sem)
+                arrive(piece(owner, c, 1), turn_near + sem)
+        tile = min(256, columns)
+
+        @pl.loop(0, columns // tile)
+        def _(t):
+            where = at(t * tile, tile, 128)
+            total = jnp.zeros((chunk, tile), jnp.float32)
+            for k in range(n_hidden * n_pair):
+                total += jnp.dot(
+                    acts_ref[k, at(c * chunk, chunk), :],
+                    down_ref[k * units : (k + 1) * units, where],
+                    preferred_element_type=jnp.float32,
+                )
+            stage_ref[at(c * chunk, chunk), where] = total.astype(jnp.bfloat16)
+
+        da, dp = steps[step]
+        for dh in range(n_hidden):
+            for de in range(n_expert):
+                offset = ((-da) % n_attn, de, dh, (-dp) % n_pair)
+                target = shifted(offset)
+                start = (c * n_hidden + target[2]) * block + target[1] * cap
+                landing = (a, group, at(e * cap, cap))
+                if any(offset):
+                    send(
+                        stage_ref.at[at(start, cap)],
+                        returned_ref.at[landing],
+                        number(*offset),
+                        target,
+                    )
+                else:
+                    returned_ref[landing] = stage_ref[at(start, cap), :]
+
+    weights[0].wait()
+    total_steps = len(steps)
+    if total_steps > 1:
+        forward(1)
+    for step in range(total_steps):
+        up(step)
+        if step + 2 < total_steps:
+            forward(step + 2)
+        if step == 0:
+            weights[1].wait()
+        if step % n_pair == n_pair - 1 and step >= 2 * n_pair - 1:
+            for earlier in range(step - 2 * n_pair + 1, step - n_pair + 1):
+                turn(earlier)
+    for step in range(max(0, total_steps - n_pair), total_steps):
+        turn(step)
+    for step in range(total_steps):
+        down(step)
+
+    for offset in others:
+        source = shifted(offset, -1)
+        arrive(
+            returned_ref.at[
+                source[0], source[2] * n_pair + source[3], at(source[1] * cap, cap)
+            ],
+            number(*offset),
+        )
+    for k in range(n_hidden * n_pair):
+        where = slice(k * columns, (k + 1) * columns)
+        total = returned_ref[0, k].astype(jnp.float32)
+        for other in range(1, n_attn):
+            total += returned_ref[other, k].astype(jnp.float32)
+        rows = total.astype(jnp.bfloat16)
+        sums = attended_ref[:, where]
+        for choice in range(2):
+            sums += share_ref[choice] * jnp.dot(
+                back_ref[choice], rows, preferred_element_type=jnp.float32
+            )
+        out_ref[0, :, where] = sums.astype(jnp.bfloat16)
+    for started in pending:
+        started.wait_send()
+
+
+def fused_body(
+    mesh,
+    queries,
+    keys,
+    values,
+    out_weight,
+    residual,
+    norm_gain,
+    route_logits,
+    expert_ids,
+    doc_lengths,
+    gate_up_weight,
+    down_weight,
+):
+    heads_out = attention(queries, keys, values, doc_lengths)
+    n_attn, n_expert, n_hidden, n_pair = (
+        mesh.shape[name] for name in ("attn", "expert", "hidden", "pair")
+    )
+    own, width = residual.shape[1:]
+    units, columns = gate_up_weight.shape[3], down_weight.shape[2]
+    cap = capacity_of(own, n_expert)
+    block = n_expert * cap
+    groups = n_hidden * n_pair
+    slots = n_attn * groups * block
+    chosen = expert_ids[0].reshape(2 * own)
+    slot_of_row = chosen * cap + rank_rows(chosen)
+    slots_of = slot_of_row.reshape(own, 2)
+    slot_ids = jnp.arange(block, dtype=jnp.int32)
+    back = (slots_of.T[:, :, None] == slot_ids[None, None, :]).astype(jnp.bfloat16)
+    pick = jnp.any(slots_of[None] == slot_ids[:, None, None], axis=2).astype(jnp.bfloat16)
+    logits = route_logits[0]
+    first_share = jax.nn.sigmoid(logits[:, 0] - logits[:, 1])
+    shares = jnp.stack([first_share, 1.0 - first_share])[:, :, None]
+    vmem = pl.BlockSpec(memory_space=pltpu.VMEM)
+    hbm = pl.BlockSpec(memory_space=pl.ANY)
+    flops = 2 * slots * (width * 2 * units + groups * units * columns)
+    return pl.pallas_call(
+        functools.partial(layer_kernel, (n_attn, n_expert, n_hidden, n_pair, own, cap)),
+        out_shape=jax.ShapeDtypeStruct(residual.shape, jnp.bfloat16),
+        in_specs=[vmem] * 7 + [hbm] * 2,
+        out_specs=vmem,
+        scratch_shapes=[
+            pltpu.VMEM(gate_up_weight.shape[1:], jnp.bfloat16),
+            pltpu.VMEM(down_weight.shape[1:], jnp.bfloat16),
+            pltpu.VMEM((n_attn * n_hidden, own, width), jnp.bfloat16),
+            pltpu.VMEM((n_attn * n_hidden, own, width), jnp.bfloat16),
+            pltpu.VMEM((own, width), jnp.float32),
+            pltpu.VMEM((block, width), jnp.bfloat16),
+            pltpu.VMEM((slots, width), jnp.bfloat16),
+            pltpu.VMEM((groups, slots, units), jnp.bfloat16),
+            pltpu.VMEM((slots, columns), jnp.bfloat16),
+            pltpu.VMEM((n_attn, groups, block, columns), jnp.bfloat16),
+            pltpu.SemaphoreType.DMA((2,)),
+            pltpu.SemaphoreType.DMA((semaphores(n_attn, n_expert, n_hidden, n_pair),)),
+            pltpu.SemaphoreType.DMA((semaphores(n_attn, n_expert, n_hidden, n_pair),)),
+        ],
+        compiler_params=pltpu.CompilerParams(
+            collective_id=0, has_side_effects=True, vmem_limit_bytes=58 * 2**20
+        ),
+        cost_estimate=pl.CostEstimate(
+            flops=flops,
+            bytes_accessed=2 * (gate_up_weight.size + down_weight.size),
+            transcendentals=slots * units,
+        ),
+    )(
+        heads_out,
+        out_weight,
+        residual,
+        norm_gain[None],
+        pick,
+        back,
+        shares,
+        gate_up_weight,
+        down_weight,
+    )
+
+
+def semaphores(n_attn, n_expert, n_hidden, n_pair):
+    chunks = n_attn * n_pair
+    return (
+        n_attn * n_hidden
+        + n_expert
+        + chunks
+        + chunks * n_hidden
+        + 2 * chunks * n_hidden
+        + 2 * chunks * n_pair
+        + 2 * chunks * n_hidden * n_pair
+        + n_attn * n_expert * n_hidden * n_pair
+    )
+
+
+def capacity_of(own, n_expert):
+    return max(2, (2 * own + n_expert - 1) // n_expert)
+
+
+def body_of(mesh, *arrays):
+    own = arrays[4].shape[1]
+    cap = capacity_of(own, mesh.shape["expert"])
+    whole_tiles = own % 16 == 0 and cap % 16 == 0
+    if whole_tiles:
+        return fused_body(mesh, *arrays)
+    return plain_body(*arrays)
+
+
 def solution(mesh):
     in_specs = (
         P(("expert", "pair"), None, ("attn", "hidden")),
@@ -131,4 +560,5 @@
         P("expert", "attn", ("hidden", "pair")),
     )
     out_specs = P(("expert", "pair"), ("attn", "hidden"), None)
+    body = functools.partial(body_of, mesh)
     return jax.shard_map(body, mesh=mesh, in_specs=in_specs, out_specs=out_specs, check_vma=False)

time: 310 us -> 161 us (0.52)
  waiting for transfers between devices: 236 us -> 0 us
  Pallas kernels: 0 us -> 150 us
  matrix products: 27.1 us -> 2.51 us
  between operations: 13.2 us -> 0.06 us
  blocking collectives: 11.6 us -> 0 us
  starting transfers between devices: 8.5 us -> 0 us
    all_gather x2 -> x0, waiting for transfers between devices: 167 us -> none  [the longest x1 88.4 us: body(): lax.all_gather(arrived, ('attn', 'hidden', 'pair'), axis=0, tiled=True)]
    pallas_call x0 -> x1, Pallas kernels: none -> 150 us  [fused_body(): pl.pallas_call(functools.partial(layer_kernel, (n_attn, n_expert, n_hidde...]
    reduce_scatter x2 -> x0, waiting for transfers between devices: 62 us -> none  [the longest x1 33.1 us: body(): lax.psum_scatter(jnp.dot(subset, out_weight, preferred_element_type=jnp.f...]
    dot_general x6 -> x2, matrix products: 27.1 us -> 2.51 us  [the longest x1 1.57 us: attention(): jnp.dot(probabilities, values[0], preferred_element_type=jnp.float32)]
    all_to_all x1 -> x0, blocking collectives: 11.6 us -> none  [body(): lax.all_to_all(outgoing, 'expert', split_axis=0, concat_axis=0, tiled=True)]
    all_to_all x1 -> x0, starting transfers between devices: 8.37 us -> none  [body(): lax.all_to_all(outgoing_wide, ('expert', 'hidden', 'pair'), split_axis=0,...]
    all_to_all x1 -> x0, waiting for transfers between devices: 7.75 us -> none  [body(): lax.all_to_all(outgoing_wide, ('expert', 'hidden', 'pair'), split_axis=0,...]
  transfers between devices with their start and end apart: 5 -> 0, of which waited for: 5 -> 0; matrix products, arithmetic and copies ran while one was open for 0% -> 0% of each run, Pallas kernels for 0% -> 0%
where the time goes in v2:
time: 161 us
  Pallas kernels  150 us (93%)
  local copies, waits for them, and re-layouts  4.28 us (3%)
  other arithmetic  4.02 us (2%)
  matrix products  2.51 us (2%)
    pallas_call x1, Pallas kernels, fused_body(): pl.pallas_call(functools.partial(layer_kernel, (n_attn, n_expert, n_hidde...  150 us

profile of v2, /device:TPU:9, one launch (start us, length us, event | category | flops | bytes accessed | tf_op | source)
XLA Modules:
  0.0 160.8 jit_solution(17671138364692339259)
XLA Ops:
  0.0 0.0 copy-start
  0.0 0.8 fusion.11
  0.8 0.1 fusion.12
  0.9 0.8 broadcast_subtract_fusion
  1.7 0.8 copy.33
  2.4 0.1 eq.59
  2.5 0.2 convert_reduce_fusion
  2.7 0.1 reduce_sum.45
  2.8 0.1 copy.35
  2.9 0.7 fusion.13
  3.6 0.7 fusion.10.back_ref
  4.3 0.1 reduce_sum.44
  4.4 0.1 copy.34
  4.4 0.7 add_bitcast_fusion
  5.1 0.1 fusion.9
  5.2 0.7 copy.36.pick_ref
  5.9 0.7 copy.37.share_ref
  6.6 0.0 copy-done
  6.6 0.9 fusion.14
  7.6 1.6 convolution_convert_fusion.heads_ref
  9.2 150.0 %shard_map.109 = bf16[1,32,4096]{2,1,0:T(8,128)(2,1)} custom-call(bf16[128,128]{1,0:T(8,128)(2,1)} %convolution_convert_fusion.heads_ref, bf16[128,4096]{1,0:T(8,128)(2,1)} %out_weight_ref.1, bf16[1,32,4096]{2,1,0:T(8,128)(2,1)} %residual_ref.1, f32[1,4096]{1,0:T(1,128)} %bitcast.30, bf16[64,32]{1,0:T(8,128)(2,1)} %copy.36.pick_ref, ...), custom_call_target="tpu_custom_call" | custom-call | flops 12884901888 | bytes 25165824 | tf_op jit(solution)/shard_map/pallas_call | solution.py:480
  159.2 1.7 %copy.39 = bf16[1,32,4096]{2,1,0:T(8,128)(2,1)} copy(bf16[1,32,4096]{2,1,0:T(8,128)(2,1)} %shard_map.109) | data formatting | bytes 524288
  (3 shorter events, 0.1 us)
Async XLA Ops:
  0.0 6.6 %copy-start = (bf16[1,128,128]{2,1,0:T(8,128)(2,1)S(1)}, bf16[1,128,128]{2,1,0:T(8,128)(2,1)}, u32[]{:S(2)}) copy-start(bf16[1,128,128]{2,1,0:T(8,128)(2,1)} %param.12) | copy-start | bytes 98308

commit v3 on v2

--- a/solution.py
+++ b/solution.py
@@ -126,20 +126,74 @@
     return layer_out.astype(jnp.bfloat16)[None]
 
 
+def attend(queries, keys, values, lengths_ref):
+    tok_group = queries.shape[0]
+    places = (tok_group, tok_group)
+    row, column = (lax.broadcasted_iota(jnp.int32, places, axis) for axis in range(2))
+    row_document, column_document = jnp.zeros(places, jnp.int32), jnp.zeros(places, jnp.int32)
+    end = 0
+    for document in range(lengths_ref.shape[1]):
+        end = end + lengths_ref[0, document]
+        row_document += (row >= end).astype(jnp.int32)
+        column_document += (column >= end).astype(jnp.int32)
+    allowed = (row_document == column_document) & (column <= row)
+    scores = lax.dot_general(
+        queries, keys, (((1,), (1,)), ((), ())), preferred_element_type=jnp.float32
+    ) * HD ** (-0.5)
+    scores = jnp.where(allowed, scores, -1e30)
+    weights = jnp.exp(scores - jnp.max(scores, axis=1, keepdims=True))
+    probabilities = (weights / jnp.sum(weights, axis=1, keepdims=True)).astype(jnp.bfloat16)
+    return jnp.dot(probabilities, values, preferred_element_type=jnp.float32).astype(
+        jnp.bfloat16
+    )
+
+
+def routing(ids_ref, logits_ref, n_expert, cap):
+    own = ids_ref.shape[2]
+    block = n_expert * cap
+    ids = [ids_ref[0, choice : choice + 1, :] for choice in range(2)]
+    experts = lax.broadcasted_iota(jnp.int32, (max(8, n_expert), own), 0)
+    named = [(experts == row).astype(jnp.float32) for row in ids]
+    row, column = (lax.broadcasted_iota(jnp.int32, (own, own), axis) for axis in range(2))
+    earlier = (row < column).astype(jnp.bfloat16)
+    before = jnp.dot(
+        (named[0] + named[1]).astype(jnp.bfloat16), earlier, preferred_element_type=jnp.float32
+    )
+    slots = [
+        one * float(cap) + jnp.sum(before * which, axis=0, keepdims=True)
+        for one, which in zip([one.astype(jnp.float32) for one in ids], named)
+    ]
+
+    def upright(values):
+        return jnp.sum(jnp.where(row == column, values, 0.0), axis=1, keepdims=True)
+
+    down_slots = lax.broadcasted_iota(jnp.int32, (block, own), 0).astype(jnp.float32)
+    across_slots = lax.broadcasted_iota(jnp.int32, (own, block), 1).astype(jnp.float32)
+    pick = sum((down_slots == slot).astype(jnp.float32) for slot in slots).astype(jnp.bfloat16)
+    back = [
+        (across_slots == upright(slot)).astype(jnp.float32).astype(jnp.bfloat16) for slot in slots
+    ]
+    first = upright(jax.nn.sigmoid(logits_ref[0, 0:1, :] - logits_ref[0, 1:2, :]))
+    return pick, back, (first, 1.0 - first)
+
+
 def layer_kernel(
     sizes,
-    heads_ref,
+    queries_ref,
+    keys_ref,
+    values_ref,
     out_weight_ref,
     residual_ref,
     gain_ref,
-    pick_ref,
-    back_ref,
-    share_ref,
+    logits_ref,
+    ids_ref,
+    lengths_ref,
     gate_up_hbm,
     down_hbm,
     out_ref,
     gate_up_ref,
     down_ref,
+    heads_ref,
     part_ref,
     sums_ref,
     attended_ref,
@@ -215,6 +269,7 @@
             device_id=dict(zip(names, shifted(offset))),
             device_id_type=pl.DeviceIdType.MESH,
         )
+    heads_ref[...] = attend(queries_ref[0], keys_ref[0], values_ref[0], lengths_ref)
     pl.semaphore_wait(barrier, len(others))
 
     used = 0
@@ -241,6 +296,7 @@
                 send(part_ref.at[slot], sums_ref.at[mine], first + slot, target)
             else:
                 attended_ref[...] = partial + residual_ref[0].astype(jnp.float32)
+    pick, back, shares = routing(ids_ref, logits_ref, n_expert, cap)
     for da in range(n_attn):
         for dh in range(n_hidden):
             if da or dh:
@@ -252,7 +308,7 @@
     scale = lax.rsqrt(jnp.mean(attended * attended, axis=1, keepdims=True) + epsilon)
     normed = (attended * scale * gain_ref[...]).astype(jnp.bfloat16)
     outgoing_ref[...] = jnp.dot(
-        pick_ref[...], normed, preferred_element_type=jnp.float32
+        pick, normed, preferred_element_type=jnp.float32
     ).astype(jnp.bfloat16)
 
     base = ((a * n_pair + p) * n_hidden + h) * block
@@ -433,8 +489,8 @@
         rows = total.astype(jnp.bfloat16)
         sums = attended_ref[:, where]
         for choice in range(2):
-            sums += share_ref[choice] * jnp.dot(
-                back_ref[choice], rows, preferred_element_type=jnp.float32
+            sums += shares[choice] * jnp.dot(
+                back[choice], rows, preferred_element_type=jnp.float32
             )
         out_ref[0, :, where] = sums.astype(jnp.bfloat16)
     for started in pending:
@@ -455,7 +511,6 @@
     gate_up_weight,
     down_weight,
 ):
-    heads_out = attention(queries, keys, values, doc_lengths)
     n_attn, n_expert, n_hidden, n_pair = (
         mesh.shape[name] for name in ("attn", "expert", "hidden", "pair")
     )
@@ -465,26 +520,19 @@
     block = n_expert * cap
     groups = n_hidden * n_pair
     slots = n_attn * groups * block
-    chosen = expert_ids[0].reshape(2 * own)
-    slot_of_row = chosen * cap + rank_rows(chosen)
-    slots_of = slot_of_row.reshape(own, 2)
-    slot_ids = jnp.arange(block, dtype=jnp.int32)
-    back = (slots_of.T[:, :, None] == slot_ids[None, None, :]).astype(jnp.bfloat16)
-    pick = jnp.any(slots_of[None] == slot_ids[:, None, None], axis=2).astype(jnp.bfloat16)
-    logits = route_logits[0]
-    first_share = jax.nn.sigmoid(logits[:, 0] - logits[:, 1])
-    shares = jnp.stack([first_share, 1.0 - first_share])[:, :, None]
     vmem = pl.BlockSpec(memory_space=pltpu.VMEM)
+    smem = pl.BlockSpec(memory_space=pltpu.SMEM)
     hbm = pl.BlockSpec(memory_space=pl.ANY)
     flops = 2 * slots * (width * 2 * units + groups * units * columns)
     return pl.pallas_call(
         functools.partial(layer_kernel, (n_attn, n_expert, n_hidden, n_pair, own, cap)),
         out_shape=jax.ShapeDtypeStruct(residual.shape, jnp.bfloat16),
-        in_specs=[vmem] * 7 + [hbm] * 2,
+        in_specs=[vmem] * 8 + [smem] + [hbm] * 2,
         out_specs=vmem,
         scratch_shapes=[
             pltpu.VMEM(gate_up_weight.shape[1:], jnp.bfloat16),
             pltpu.VMEM(down_weight.shape[1:], jnp.bfloat16),
+            pltpu.VMEM(queries.shape[1:], jnp.bfloat16),
             pltpu.VMEM((n_attn * n_hidden, own, width), jnp.bfloat16),
             pltpu.VMEM((n_attn * n_hidden, own, width), jnp.bfloat16),
             pltpu.VMEM((own, width), jnp.float32),
@@ -506,13 +554,15 @@
             transcendentals=slots * units,
         ),
     )(
-        heads_out,
+        queries,
+        keys,
+        values,
         out_weight,
         residual,
         norm_gain[None],
-        pick,
-        back,
-        shares,
+        route_logits.transpose(0, 2, 1),
+        expert_ids.transpose(0, 2, 1),
+        doc_lengths,
         gate_up_weight,
         down_weight,
     )

time: 161 us -> 152 us (0.944)
  other arithmetic: 4.02 us -> 0 us
  local copies, waits for them, and re-layouts: 4.28 us -> 1.67 us
  matrix products: 2.51 us -> 0 us
    dot_general x2 -> x0, matrix products: 2.51 us -> none  [the longest x1 1.57 us: attention(): jnp.dot(probabilities, values[0], preferred_element_type=jnp.float32)]
where the time goes in v3:
time: 152 us
  Pallas kernels  150 us (99%)
  local copies, waits for them, and re-layouts  1.67 us (1%)
    pallas_call x1, Pallas kernels, fused_body(): pl.pallas_call(functools.partial(layer_kernel, (n_attn, n_expert, n_hidde...  150 us

profile of v3, /device:TPU:9, one launch (start us, length us, event | category | flops | bytes accessed | tf_op | source)
XLA Modules:
  0.0 151.9 jit_solution(18120084941501345905)
XLA Ops:
  0.0 150.2 %shard_map.109 = bf16[1,32,4096]{2,1,0:T(8,128)(2,1)} custom-call(bf16[1,128,128]{2,1,0:T(8,128)(2,1)} %queries_ref.1, bf16[1,128,128]{2,1,0:T(8,128)(2,1)} %keys_ref.1, bf16[1,128,128]{2,1,0:T(8,128)(2,1)} %values_ref.1, bf16[128,4096]{1,0:T(8,128)(2,1)} %out_weight_ref.1, bf16[1,32,4096]{2,1,0:T(8,128)(2,1)} %residual_ref.1, f32[1,4096]{1,0:T(1,128)} %bitcast.3, ...), custom_call_target="tpu_custom_call" | custom-call | flops 12884901888 | bytes 25165824 | tf_op jit(solution)/shard_map/pallas_call | solution.py:527
  150.2 1.7 %copy.13 = bf16[1,32,4096]{2,1,0:T(8,128)(2,1)} copy(bf16[1,32,4096]{2,1,0:T(8,128)(2,1)} %shard_map.109) | data formatting | bytes 524288

commit v4 on v3

--- a/solution.py
+++ b/solution.py
@@ -195,6 +195,8 @@
     down_ref,
     heads_ref,
     part_ref,
+    landed_ref,
+    halfway_ref,
     sums_ref,
     attended_ref,
     outgoing_ref,
@@ -217,7 +219,7 @@
     block = n_expert * cap
     chunk = n_hidden * block
     chunks = n_attn * n_pair
-    half = chunk // 2
+    early = (chunk * 3 // 4) // 16 * 16
     pending = []
 
     def shifted(offset, sign=1):
@@ -279,31 +281,60 @@
         used += count
         return used - count
 
-    first = numbers(n_attn * n_hidden)
-    mine = a * n_hidden + h
-    for da in reversed(range(n_attn)):
-        for dh in reversed(range(n_hidden)):
-            target = shifted((da, 0, dh, 0))
-            owner = target[0] * n_hidden + target[2]
-            partial = jnp.dot(
-                heads_ref[at(owner * own, own), :],
-                out_weight_ref[...],
-                preferred_element_type=jnp.float32,
+    bands = 4 if width % 512 == 0 else 1
+    band = width // bands
+    over_hidden = numbers(bands * n_hidden)
+    over_attn = numbers(bands * n_attn)
+
+    def partial(row, column, where):
+        return jnp.dot(
+            heads_ref[at((row * n_hidden + column) * own, own), :],
+            out_weight_ref[:, where],
+            preferred_element_type=jnp.float32,
+        )
+
+    places = [slice(j * band, (j + 1) * band) for j in range(bands)]
+    for j, where in enumerate(places):
+        for dh in range(1, n_hidden):
+            target = shifted((0, 0, dh, 0))
+            for row in range(n_attn):
+                part_ref[dh, row * own : (row + 1) * own, where] = partial(
+                    row, target[2], where
+                ).astype(jnp.bfloat16)
+            send(
+                part_ref.at[dh, :, where],
+                landed_ref.at[h, :, where],
+                over_hidden + j * n_hidden + dh,
+                target,
             )
-            if da or dh:
-                slot = da * n_hidden + dh
-                part_ref[slot] = partial.astype(jnp.bfloat16)
-                send(part_ref.at[slot], sums_ref.at[mine], first + slot, target)
+    pick, back, shares = routing(ids_ref, logits_ref, n_expert, cap)
+    for j, where in enumerate(places):
+        for dh in range(1, n_hidden):
+            source = shifted((0, 0, dh, 0), -1)
+            arrive(landed_ref.at[source[2], :, where], over_hidden + j * n_hidden + dh)
+        for da in reversed(range(n_attn)):
+            target = shifted((da, 0, 0, 0))
+            total = partial(target[0], h, where)
+            for dh in range(1, n_hidden):
+                source = shifted((0, 0, dh, 0), -1)
+                total += landed_ref[source[2], at(target[0] * own, own), where].astype(
+                    jnp.float32
+                )
+            if da:
+                halfway_ref[da, :, where] = total.astype(jnp.bfloat16)
+                send(
+                    halfway_ref.at[da, :, where],
+                    sums_ref.at[a, :, where],
+                    over_attn + j * n_attn + da,
+                    target,
+                )
             else:
-                attended_ref[...] = partial + residual_ref[0].astype(jnp.float32)
-    pick, back, shares = routing(ids_ref, logits_ref, n_expert, cap)
-    for da in range(n_attn):
-        for dh in range(n_hidden):
-            if da or dh:
-                source = shifted((da, 0, dh, 0), -1)
-                slot = source[0] * n_hidden + source[2]
-                arrive(sums_ref.at[slot], first + da * n_hidden + dh)
-                attended_ref[...] += sums_ref[slot].astype(jnp.float32)
+                attended_ref[:, where] = total + residual_ref[0, :, where].astype(jnp.float32)
+    for j, where in enumerate(places):
+        for da in range(1, n_attn):
+            source = shifted((da, 0, 0, 0), -1)
+            arrive(sums_ref.at[source[0], :, where], over_attn + j * n_attn + da)
+            attended_ref[:, where] += sums_ref[source[0], :, where].astype(jnp.float32)
     attended = attended_ref[...]
     scale = lax.rsqrt(jnp.mean(attended * attended, axis=1, keepdims=True) + epsilon)
     normed = (attended * scale * gain_ref[...]).astype(jnp.bfloat16)
@@ -326,7 +357,7 @@
         source = shifted((0, de, 0, 0), -1)
         arrive(rows_ref.at[at(base + source[1] * cap, cap)], first + de)
 
-    steps = [(da, dp) for da in range(n_attn) for dp in range(n_pair)]
+    steps = [(da, dp) for da in reversed(range(n_attn)) for dp in reversed(range(n_pair))]
     along = numbers(chunks)
     across = numbers(chunks * n_hidden)
 
@@ -336,9 +367,9 @@
             send(block_ref, block_ref, across + step * n_hidden + dh, shifted((0, 0, dh, 0)))
 
     own_rows = rows_ref.at[at(base, block)]
-    spread(0, base)
+    spread(chunks - 1, base)
     for step, (da, dp) in enumerate(steps):
-        if step:
+        if da or dp:
             send(own_rows, own_rows, along + step, shifted((da, 0, 0, dp)))
 
     def chunk_of(step):
@@ -358,7 +389,7 @@
     group = h * n_pair + p
 
     def piece(owner, c, part):
-        return acts_ref.at[owner, at(c * chunk + part * half, half)]
+        return acts_ref.at[owner, at(c * chunk + part * early, chunk - early if part else early)]
 
     def up(step):
         c = chunk_of(step)
@@ -456,21 +487,19 @@
                     returned_ref[landing] = stage_ref[at(start, cap), :]
 
     weights[0].wait()
-    total_steps = len(steps)
-    if total_steps > 1:
-        forward(1)
-    for step in range(total_steps):
+    for step in range(chunks - 1):
+        if step < 2:
+            forward(step)
+    for step in range(chunks):
         up(step)
-        if step + 2 < total_steps:
+        if step + 2 < chunks - 1:
             forward(step + 2)
-        if step == 0:
-            weights[1].wait()
-        if step % n_pair == n_pair - 1 and step >= 2 * n_pair - 1:
-            for earlier in range(step - 2 * n_pair + 1, step - n_pair + 1):
-                turn(earlier)
-    for step in range(max(0, total_steps - n_pair), total_steps):
+    weights[1].wait()
+    for step in range(chunks):
         turn(step)
-    for step in range(total_steps):
+        if step >= n_pair:
+            down(step - n_pair)
+    for step in range(max(0, chunks - n_pair), chunks):
         down(step)
 
     for offset in others:
@@ -533,8 +562,10 @@
             pltpu.VMEM(gate_up_weight.shape[1:], jnp.bfloat16),
             pltpu.VMEM(down_weight.shape[1:], jnp.bfloat16),
             pltpu.VMEM(queries.shape[1:], jnp.bfloat16),
-            pltpu.VMEM((n_attn * n_hidden, own, width), jnp.bfloat16),
-            pltpu.VMEM((n_attn * n_hidden, own, width), jnp.bfloat16),
+            pltpu.VMEM((n_hidden, n_attn * own, width), jnp.bfloat16),
+            pltpu.VMEM((n_hidden, n_attn * own, width), jnp.bfloat16),
+            pltpu.VMEM((n_attn, own, width), jnp.bfloat16),
+            pltpu.VMEM((n_attn, own, width), jnp.bfloat16),
             pltpu.VMEM((own, width), jnp.float32),
             pltpu.VMEM((block, width), jnp.bfloat16),
             pltpu.VMEM((slots, width), jnp.bfloat16),
@@ -571,7 +602,8 @@
 def semaphores(n_attn, n_expert, n_hidden, n_pair):
     chunks = n_attn * n_pair
     return (
-        n_attn * n_hidden
+        4 * n_hidden
+        + 4 * n_attn
         + n_expert
         + chunks
         + chunks * n_hidden

time: 152 us -> 167 us (1.099); the launches traced: 152 us -> 165 us
  Pallas kernels: 150 us -> 163 us
    pallas_call x1, Pallas kernels: 150 us -> 163 us  [fused_body(): pl.pallas_call(functools.partial(layer_kernel, (n_attn, n_expert, n_hidde...]
where the time goes in v4:
time: 167 us; the launch traced here: 165 us
  Pallas kernels  163 us (98%)
  local copies, waits for them, and re-layouts  1.67 us (1%)
    pallas_call x1, Pallas kernels, fused_body(): pl.pallas_call(functools.partial(layer_kernel, (n_attn, n_expert, n_hidde...  163 us

profile of v4, /device:TPU:9, one launch (start us, length us, event | category | flops | bytes accessed | tf_op | source)
XLA Modules:
  0.0 164.6 jit_solution(12691824480918487731)
XLA Ops:
  0.0 162.9 %shard_map.109 = bf16[1,32,4096]{2,1,0:T(8,128)(2,1)} custom-call(bf16[1,128,128]{2,1,0:T(8,128)(2,1)} %queries_ref.1, bf16[1,128,128]{2,1,0:T(8,128)(2,1)} %keys_ref.1, bf16[1,128,128]{2,1,0:T(8,128)(2,1)} %values_ref.1, bf16[128,4096]{1,0:T(8,128)(2,1)} %out_weight_ref.1, bf16[1,32,4096]{2,1,0:T(8,128)(2,1)} %residual_ref.1, f32[1,4096]{1,0:T(1,128)} %bitcast.3, ...), custom_call_target="tpu_custom_call" | custom-call | flops 12884901888 | bytes 25165824 | tf_op jit(solution)/shard_map/pallas_call | solution.py:556
  162.9 1.7 %copy.13 = bf16[1,32,4096]{2,1,0:T(8,128)(2,1)} copy(bf16[1,32,4096]{2,1,0:T(8,128)(2,1)} %shard_map.109) | data formatting | bytes 524288

commit v5 on v4

--- a/solution.py
+++ b/solution.py
@@ -219,7 +219,7 @@
     block = n_expert * cap
     chunk = n_hidden * block
     chunks = n_attn * n_pair
-    early = (chunk * 3 // 4) // 16 * 16
+    half = chunk // 2
     pending = []
 
     def shifted(offset, sign=1):
@@ -357,7 +357,7 @@
         source = shifted((0, de, 0, 0), -1)
         arrive(rows_ref.at[at(base + source[1] * cap, cap)], first + de)
 
-    steps = [(da, dp) for da in reversed(range(n_attn)) for dp in reversed(range(n_pair))]
+    steps = [(da, dp) for da in range(n_attn) for dp in range(n_pair)]
     along = numbers(chunks)
     across = numbers(chunks * n_hidden)
 
@@ -367,9 +367,9 @@
             send(block_ref, block_ref, across + step * n_hidden + dh, shifted((0, 0, dh, 0)))
 
     own_rows = rows_ref.at[at(base, block)]
-    spread(chunks - 1, base)
+    spread(0, base)
     for step, (da, dp) in enumerate(steps):
-        if da or dp:
+        if step:
             send(own_rows, own_rows, along + step, shifted((da, 0, 0, dp)))
 
     def chunk_of(step):
@@ -389,7 +389,7 @@
     group = h * n_pair + p
 
     def piece(owner, c, part):
-        return acts_ref.at[owner, at(c * chunk + part * early, chunk - early if part else early)]
+        return acts_ref.at[owner, at(c * chunk + part * half, half)]
 
     def up(step):
         c = chunk_of(step)
@@ -487,19 +487,21 @@
                     returned_ref[landing] = stage_ref[at(start, cap), :]
 
     weights[0].wait()
-    for step in range(chunks - 1):
-        if step < 2:
-            forward(step)
-    for step in range(chunks):
+    total_steps = len(steps)
+    if total_steps > 1:
+        forward(1)
+    for step in range(total_steps):
         up(step)
-        if step + 2 < chunks - 1:
+        if step + 2 < total_steps:
             forward(step + 2)
-    weights[1].wait()
-    for step in range(chunks):
+        if step == 0:
+            weights[1].wait()
+        if step % n_pair == n_pair - 1 and step >= 2 * n_pair - 1:
+            for earlier in range(step - 2 * n_pair + 1, step - n_pair + 1):
+                turn(earlier)
+    for step in range(max(0, total_steps - n_pair), total_steps):
         turn(step)
-        if step >= n_pair:
-            down(step - n_pair)
-    for step in range(max(0, chunks - n_pair), chunks):
+    for step in range(total_steps):
         down(step)
 
     for offset in others:

time: 167 us -> 151 us (0.904); the launches traced: 165 us -> 150 us
  Pallas kernels: 163 us -> 149 us
    pallas_call x1, Pallas kernels: 163 us -> 149 us  [fused_body(): pl.pallas_call(functools.partial(layer_kernel, (n_attn, n_expert, n_hidde...]
where the time goes in v5:
time: 151 us; the launch traced here: 150 us
  Pallas kernels  149 us (99%)
  local copies, waits for them, and re-layouts  1.67 us (1%)
    pallas_call x1, Pallas kernels, fused_body(): pl.pallas_call(functools.partial(layer_kernel, (n_attn, n_expert, n_hidde...  149 us

profile of v5, /device:TPU:9, one launch (start us, length us, event | category | flops | bytes accessed | tf_op | source)
XLA Modules:
  0.0 150.4 jit_solution(2786040713897977125)
XLA Ops:
  0.0 148.7 %shard_map.109 = bf16[1,32,4096]{2,1,0:T(8,128)(2,1)} custom-call(bf16[1,128,128]{2,1,0:T(8,128)(2,1)} %queries_ref.1, bf16[1,128,128]{2,1,0:T(8,128)(2,1)} %keys_ref.1, bf16[1,128,128]{2,1,0:T(8,128)(2,1)} %values_ref.1, bf16[128,4096]{1,0:T(8,128)(2,1)} %out_weight_ref.1, bf16[1,32,4096]{2,1,0:T(8,128)(2,1)} %residual_ref.1, f32[1,4096]{1,0:T(1,128)} %bitcast.3, ...), custom_call_target="tpu_custom_call" | custom-call | flops 12884901888 | bytes 25165824 | tf_op jit(solution)/shard_map/pallas_call | solution.py:558
  148.7 1.7 %copy.13 = bf16[1,32,4096]{2,1,0:T(8,128)(2,1)} copy(bf16[1,32,4096]{2,1,0:T(8,128)(2,1)} %shard_map.109) | data formatting | bytes 524288
